TPU v7x, 32 devices: a whole 2x2x4 slice. The times are simulated.
32 devices in a mesh: expert: 32 (over z, y, x, core).
Axes of the slice: x: 2, y: 2, z: 4, core: 2. Of those that a mesh axis runs over, the one named last changes fastest.
Arguments:
- tokens: bfloat16 [4096, 4096], P('expert'), may hold values from -6 to 6
- norm_gain: float32 [4096], replicated, may hold values from 0.5 to 1.5
- router_weight: bfloat16 [4096, 32], replicated, may hold values from -0.09375 to 0.09375
- expert_ids: int32 [4096, 2], P('expert'), may hold values from 0 to 31, as said below
- gate_proj: bfloat16 [32, 4096, 768], P('expert'), may hold values from -0.09375 to 0.09375
- up_proj: bfloat16 [32, 4096, 768], P('expert'), may hold values from -0.09375 to 0.09375
- down_proj: bfloat16 [32, 768, 4096], P('expert'), may hold values from -0.21875 to 0.21875
- value_weight: bfloat16 [4096], replicated, may hold values from -0.09375 to 0.09375
- value_target: int32 [4096], P('expert'), may hold values from -1 to 1
- recency: float32 [4096], P('expert'), may hold values from 0.25 to 18, as said below
Outputs:
- mixed: bfloat16 [4096, 4096], P('expert')
- values: float32 [4096], P('expert')
- loss: float32 [], replicated
Inputs may be any that keep to these rules, and one draw needn't show every extreme that they name: `expert_ids`: each row names two different experts; among the rows of one device no expert is named more than 12 times. `recency`: positive weights.
All inputs are finite; a program needn't handle non-finite values.
Results may differ from a plain program's by a relative error of at most 0.0055.
Values may be sent and summed in bfloat16 or wider, within the bound.
A program may use at most 128 MiB of HBM per device.

v0:
```python
import jax
import jax.numpy as jnp
from jax import lax
from jax.sharding import PartitionSpec as P


def expert_ffn(received, gate_proj, up_proj, down_proj):
    sources, slots, width = received.shape
    flat_input = received.reshape(sources * slots, width)
    gate_part = jnp.dot(flat_input, gate_proj[0], preferred_element_type=jnp.float32)
    up_part = jnp.dot(flat_input, up_proj[0], preferred_element_type=jnp.float32)
    hidden = (jax.nn.silu(gate_part) * up_part).astype(jnp.bfloat16)
    result = jnp.dot(hidden, down_proj[0], preferred_element_type=jnp.float32).astype(jnp.bfloat16)
    return result.reshape(sources, slots, width)


def body(
    tokens,
    norm_gain,
    router_weight,
    expert_ids,
    gate_proj,
    up_proj,
    down_proj,
    value_weight,
    value_target,
    recency,
):
    token_count, width = tokens.shape
    expert_total = router_weight.shape[1]
    capacity = 3 * token_count // expert_total
    wide = tokens.astype(jnp.float32)
    inverse = lax.rsqrt(jnp.mean(wide * wide, axis=1, keepdims=True) + 1e-05)
    normed = (wide * inverse * norm_gain).astype(jnp.bfloat16)
    logits = jnp.dot(normed, router_weight, preferred_element_type=jnp.float32)
    columns = lax.broadcasted_iota(jnp.int32, (1, expert_total), 1)
    first = jnp.sum(jnp.where(expert_ids[:, 0:1] == columns, logits, 0.0), axis=1)
    second = jnp.sum(jnp.where(expert_ids[:, 1:2] == columns, logits, 0.0), axis=1)
    gate_first = jax.nn.sigmoid(first - second)
    gate_second = jax.nn.sigmoid(second - first)
    flat_ids = expert_ids.reshape(-1)
    one_hot = (flat_ids[:, None] == columns).astype(jnp.int32)
    slot_rank = jnp.sum(jnp.cumsum(one_hot, axis=0) * one_hot, axis=1) - 1
    slot_index = flat_ids * capacity + slot_rank
    row_index = jnp.arange(2 * token_count, dtype=jnp.int32) // 2
    source_row = (
        jnp.full((expert_total * capacity,), token_count, dtype=jnp.int32)
        .at[slot_index]
        .set(row_index)
    )
    padded = jnp.concatenate([normed, jnp.zeros((1, width), jnp.bfloat16)], axis=0)
    outgoing = padded[source_row].reshape(expert_total, capacity, width)
    received = lax.all_to_all(outgoing, "expert", split_axis=0, concat_axis=0, tiled=True)
    produced = expert_ffn(received, gate_proj, up_proj, down_proj)
    returned = lax.all_to_all(produced, "expert", split_axis=0, concat_axis=0, tiled=True)
    flat_back = returned.reshape(expert_total * capacity, width)
    picked = flat_back[slot_index].reshape(token_count, 2, width)
    mixed = (
        wide
        + gate_first[:, None] * picked[:, 0].astype(jnp.float32)
        + gate_second[:, None] * picked[:, 1].astype(jnp.float32)
    ).astype(jnp.bfloat16)
    values = jnp.tanh(jnp.dot(mixed, value_weight, preferred_element_type=jnp.float32))
    error = values - value_target.astype(jnp.float32)
    weighted, weight_total = lax.psum(
        (jnp.sum(recency * error * error), jnp.sum(recency)), "expert"
    )
    loss = weighted / weight_total
    return (mixed, values, loss)


def solution(mesh):
    return jax.shard_map(
        body,
        mesh=mesh,
        in_specs=(
            P("expert", None),
            P(),
            P(),
            P("expert", None),
            P("expert", None, None),
            P("expert", None, None),
            P("expert", None, None),
            P(),
            P("expert"),
            P("expert"),
        ),
        out_specs=(P("expert", None), P("expert"), P()),
        check_vma=False,
    )
```

profile of v0, /device:TPU:0, one launch (start us, length us, event | category | flops | bytes accessed | tf_op | source)
XLA Modules:
  0.0 310.4 jit_solution(15629568829031750835)
XLA Ops:
  0.6 0.0 copy-start
  0.6 0.0 copy-start.1
  0.7 0.8 broadcast_multiply_fusion
  1.4 0.8 copy.14
  2.2 0.1 eq.67
  2.4 0.1 eq.63
  2.5 1.5 fusion.9
  4.0 0.1 copy.13
  4.2 0.1 mul.75
  4.3 0.6 reduce-window.6
  4.9 0.2 slice_reduce_fusion
  5.1 0.1 fusion.25
  5.3 1.4 scatter_custom_fusion
  6.7 0.0 copy-done.1
  6.7 1.0 fusion.11
  7.8 0.1 concatenate.3
  7.9 4.1 %gather_fusion = bf16[384,4096]{1,0:T(8,128)(2,1)} fusion(bf16[129,4096]{1,0:T(8,128)(2,1)S(1)} %concatenate.3, s32[1024]{0:T(1024)S(1)} %pad_clamp_fusion.1), kind=kCustom, calls=%fused_computation | custom fusion | bytes 6292992 | tf_op jit(solution)/shard_map/gather | solution.py:52
  11.9 5.5 %reshape.104 = bf16[32,12,4096]{2,1,0:T(8,128)(2,1)} reshape(bf16[384,4096]{1,0:T(8,128)(2,1)} %gather_fusion) | data formatting | bytes 6291456 | tf_op jit(solution)/shard_map/reshape | solution.py:52
  17.4 101.1 %all_to_all.10 = bf16[32,12,4096]{2,1,0:T(8,128)(2,1)} all-to-all(bf16[32,12,4096]{2,1,0:T(8,128)(2,1)} %reshape.104), channel_id=1, replica_groups=mesh['expert'=32] {'expert'}, dimensions={0} | all-to-all | bytes 6291456 | tf_op jit(solution)/shard_map/all_to_all | solution.py:53
  118.5 5.6 %reshape.105 = bf16[384,4096]{1,0:T(8,128)(2,1)} reshape(bf16[32,12,4096]{2,1,0:T(8,128)(2,1)} %all_to_all.10) | data formatting | bytes 6291456 | tf_op jit(solution)/shard_map/reshape | solution.py:9
  124.1 7.4 %fusion.4 = f32[384,768]{1,0:T(8,128)} fusion(bf16[384,4096]{1,0:T(8,128)(2,1)} %reshape.105, bf16[1,4096,768]{2,1,0:T(8,128)(2,1)} %param.14), kind=kOutput, calls=%fused_computation.7 | convolution fusion | flops 2415919104 | bytes 10616832 | tf_op jit(solution)/shard_map/dot_general | solution.py:10
  131.5 14.2 %fusion.6 = bf16[384,4096]{1,0:T(8,128)(2,1)} fusion(bf16[1,768,4096]{2,1,0:T(8,128)(2,1)} %param.16, bf16[384,4096]{1,0:T(8,128)(2,1)} %reshape.105, bf16[1,4096,768]{2,1,0:T(8,128)(2,1)} %param.15, f32[384,768]{1,0:T(8,128)} %fusion.4), kind=kOutput, calls=%fused_computation.9 | convolution fusion | flops 4835180544 | bytes 20054016 | tf_op jit(solution)/shard_map/dot_general | solution.py:13
  145.7 5.5 %reshape.106 = bf16[32,12,4096]{2,1,0:T(8,128)(2,1)} reshape(bf16[384,4096]{1,0:T(8,128)(2,1)} %fusion.6) | data formatting | bytes 6291456 | tf_op jit(solution)/shard_map/reshape | solution.py:14
  151.2 0.0 copy-start.5
  151.2 0.0 copy-start.4
  151.2 4.0 %all-to-all-start.1 = ((bf16[32,12,4096]{2,1,0:T(8,128)(2,1)}), bf16[32,12,4096]{2,1,0:T(8,128)(2,1)}, u32[]{:S(2)}, u32[]{:S(2)}) async-start(bf16[32,12,4096]{2,1,0:T(8,128)(2,1)} %reshape.106), calls=%async_computation.1 | async-start | bytes 8388608 | tf_op jit(solution)/shard_map/all_to_all | solution.py:55
  155.2 0.0 copy-done.5
  155.2 0.0 copy-done.4
  155.3 0.0 copy-done
  155.3 0.5 select_reduce_fusion.1
  155.8 93.2 %all-to-all-done.1 = bf16[32,12,4096]{2,1,0:T(8,128)(2,1)} async-done(((bf16[32,12,4096]{2,1,0:T(8,128)(2,1)}), bf16[32,12,4096]{2,1,0:T(8,128)(2,1)}, u32[]{:S(2)}, u32[]{:S(2)}) %all-to-all-start.1) | async-done | bytes 3145760 | tf_op jit(solution)/shard_map/all_to_all | solution.py:55
  249.0 4.0 %reshape.107 = bf16[384,4096]{1,0:T(8,128)(2,1)S(1)} reshape(bf16[32,12,4096]{2,1,0:T(8,128)(2,1)} %all-to-all-done.1) | data formatting | bytes 6291456 | tf_op jit(solution)/shard_map/reshape | solution.py:56
  253.0 3.2 %gather_fusion.1 = bf16[256,4096]{1,0:T(8,128)(2,1)} fusion(bf16[384,4096]{1,0:T(8,128)(2,1)S(1)} %reshape.107, s32[1024]{0:T(1024)S(1)} %pad_clamp_fusion), kind=kCustom, calls=%fused_computation.1 | custom fusion | bytes 4195328 | tf_op jit(solution)/shard_map/gather | solution.py:57
  256.2 3.2 %reshape.108 = bf16[128,2,4096]{2,1,0:T(2,128)(2,1)S(1)} reshape(bf16[256,4096]{1,0:T(8,128)(2,1)} %gather_fusion.1) | data formatting | bytes 4194304 | tf_op jit(solution)/shard_map/reshape | solution.py:57
  259.3 0.0 copy-start.2
  259.4 4.7 %fusion.32 = (bf16[128,1,4096]{2,1,0:T(2,128)(2,1)S(1)}, bf16[128,1,4096]{2,1,0:T(2,128)(2,1)S(1)}) fusion(bf16[128,2,4096]{2,1,0:T(2,128)(2,1)S(1)} %reshape.108), kind=kLoop, calls=%fused_computation.60 | loop fusion | bytes 4194304 | tf_op jit(solution)/shard_map/slice | solution.py:60
  264.0 0.0 copy-done.2
  264.1 0.0 copy-start.6
  264.1 0.0 copy-start.7
  264.1 4.2 %fusion.13 = bf16[128,4096]{1,0:T(8,128)(2,1)S(1)} fusion(bf16[128,4096]{1,0:T(8,128)(2,1)S(1)} %copy-done.2, bf16[128,1,4096]{2,1,0:T(2,128)(2,1)S(1)} %get-tuple-element.10, bf16[128,1,4096]{2,1,0:T(2,128)(2,1)S(1)} %get-tuple-element.9, f32[128]{0:T(128)S(1)} %get-tuple-element.12, f32[128]{0:T(128)S(1)} %get-tuple-element.11), kind=kLoop, calls=%fused_computation.17 | loop fusion | flops 4194304 | bytes 4195328 | tf_op jit(solution)/shard_map/convert_element_type | solution.py:62
  268.3 0.0 copy-done.6
  268.3 0.0 copy-done.7
  268.3 0.0 copy-start.3
  268.3 1.6 fusion.31
  269.9 38.2 %all-reduce.1 = (f32[]{:T(128)}, f32[]{:T(128)}) all-reduce(f32[]{:T(128)} %get-tuple-element.6, f32[]{:T(128)} %get-tuple-element.5), channel_id=1, replica_groups=mesh['expert'=32] {'expert'}, use_global_device_ids=true, to_apply=%region_8.9 | all-reduce | flops 2 | bytes 16 | tf_op jit(solution)/shard_map/psum | solution.py:65
  309.3 0.0 copy-done.3
  (13 shorter events, 0.1 us)
Async XLA Ops:
  0.6 154.6 %copy-start = (bf16[4096,32]{0,1:T(8,128)(2,1)S(1)}, bf16[4096,32]{0,1:T(8,128)(2,1)}, u32[]{:S(2)}) copy-start(bf16[4096,32]{0,1:T(8,128)(2,1)} %param.12) | copy-start | bytes 786436
  0.6 6.1 %copy-start.1 = (bf16[128,4096]{1,0:T(8,128)(2,1)S(1)}, bf16[128,4096]{1,0:T(8,128)(2,1)}, u32[]{:S(2)}) copy-start(bf16[128,4096]{1,0:T(8,128)(2,1)} %param.10) | copy-start | bytes 3145732
  151.2 4.0 %copy-start.5 = (bf16[4096]{0:T(1024)(128)(2,1)S(1)}, bf16[4096]{0:T(1024)(128)(2,1)}, u32[]{:S(2)}) copy-start(bf16[4096]{0:T(1024)(128)(2,1)} %param.17) | copy-start | bytes 24580
  151.2 4.1 %copy-start.4 = (s32[128,2]{0,1:T(2,128)S(1)}, s32[128,2]{0,1:T(2,128)}, u32[]{:S(2)}) copy-start(s32[128,2]{0,1:T(2,128)} %param.13) | copy-start | bytes 3076
  151.2 97.8 %all-to-all-start.1 = ((bf16[32,12,4096]{2,1,0:T(8,128)(2,1)}), bf16[32,12,4096]{2,1,0:T(8,128)(2,1)}, u32[]{:S(2)}, u32[]{:S(2)}) async-start(bf16[32,12,4096]{2,1,0:T(8,128)(2,1)} %reshape.106), calls=%async_computation.1 | async-start | bytes 8388608 | tf_op jit(solution)/shard_map/all_to_all | solution.py:55
  259.3 4.7 %copy-start.2 = (bf16[128,4096]{1,0:T(8,128)(2,1)S(1)}, bf16[128,4096]{1,0:T(8,128)(2,1)}, u32[]{:S(2)}) copy-start(bf16[128,4096]{1,0:T(8,128)(2,1)} %param.10) | copy-start | bytes 3145732
  264.1 4.2 %copy-start.6 = (f32[128]{0:T(128)S(1)}, f32[128]{0:T(128)}, u32[]{:S(2)}) copy-start(f32[128]{0:T(128)} %param.19) | copy-start | bytes 1540
  264.1 4.2 %copy-start.7 = (s32[128]{0:T(128)S(1)}, s32[128]{0:T(128)}, u32[]{:S(2)}) copy-start(s32[128]{0:T(128)} %param.18) | copy-start | bytes 1540
  268.3 41.0 %copy-start.3 = (bf16[128,4096]{1,0:T(8,128)(2,1)}, bf16[128,4096]{1,0:T(8,128)(2,1)S(1)}, u32[]{:S(2)}) copy-start(bf16[128,4096]{1,0:T(8,128)(2,1)S(1)} %fusion.13) | copy-start | bytes 3145732
where the time goes:
time: 312 us; the launch traced here: 310 us
  blocking collectives  139 us (45%)
  waiting for transfers between devices  93.2 us (30%)
  local copies, waits for them, and re-layouts  38.7 us (12%)
  matrix products  23.6 us (8%)
  other arithmetic  8.31 us (3%)
  starting transfers between devices  4.02 us (1%)
  between operations  3.28 us (1%)
    all_to_all x1, blocking collectives, body(): lax.all_to_all(outgoing, 'expert', split_axis=0, concat_axis=0, tiled=True)  101 us
    all_to_all x1, waiting for transfers between devices, body(): lax.all_to_all(produced, 'expert', split_axis=0, concat_axis=0, tiled=True)  93.2 us
    psum x1, blocking collectives, body(): lax.psum((jnp.sum(recency * error * error), jnp.sum(recency)), 'expert')  38.2 us
    dot_general x1, matrix products, expert_ffn(): jnp.dot(hidden, down_proj[0], preferred_element_type=jnp.float32)  14.2 us
    dot_general x1, matrix products, expert_ffn(): jnp.dot(flat_input, gate_proj[0], preferred_element_type=jnp.float32)  7.38 us
  transfers between devices with their start and end apart: 1, of which 1 were waited for; matrix products, arithmetic and copies ran while one was open for 0% of the time, Pallas kernels for 0%

commit v1 on v0

v1 whole, which is shorter than its diff:
```python
import functools

import jax
import jax.numpy as jnp
import numpy as np
from jax import lax
from jax.experimental import pallas as pl
from jax.experimental.pallas import tpu as pltpu
from jax.sharding import PartitionSpec as P

BLOCKS = 4
MESH = pl.DeviceIdType.MESH
F32 = jnp.float32
BF16 = jnp.bfloat16


def to_column(row):
    t = row.shape[1]
    shape = (t, t)
    eye = lax.broadcasted_iota(jnp.int32, shape, 0) == lax.broadcasted_iota(jnp.int32, shape, 1)
    return jnp.sum(jnp.where(eye, row, 0.0), axis=1, keepdims=True)


def to_row(column):
    t = column.shape[0]
    shape = (t, t)
    eye = lax.broadcasted_iota(jnp.int32, shape, 0) == lax.broadcasted_iota(jnp.int32, shape, 1)
    return jnp.sum(jnp.where(eye, column, 0.0), axis=0, keepdims=True)


def kernel(
    axis, n, cap, parts,
    tok_ref, gain_ref, router_ref, ids_ref, head_ref, target_ref, recency_ref, split_ref, merge_ref,
    gate_hbm, up_hbm, down_hbm,
    mixed_ref, values_ref, loss_ref,
    gate_v, up_v, down_v, normed, send, recv, xs, ys, yout, ret, acc, sums, all_sums,
    w_sem, s1, r1, s2, r2, s3, r3,
):
    tokens, width = tok_ref.shape
    part = width // parts
    per = n // BLOCKS
    rows = per * cap * parts
    flat = per * cap
    me = lax.axis_index(axis)
    mine, place = me // per, lax.rem(me, per)

    def block_of(h):
        high = lax.rem(mine // 2 + h // 2, 2)
        low = lax.rem(lax.rem(mine, 2) + lax.rem(h, 2), 2)
        return 2 * high + low

    weights = [
        pltpu.make_async_copy(gate_hbm.at[0], gate_v, w_sem.at[0]),
        pltpu.make_async_copy(up_hbm.at[0], up_v, w_sem.at[1]),
        pltpu.make_async_copy(down_hbm.at[0], down_v, w_sem.at[2]),
    ]
    barrier = pltpu.get_barrier_semaphore()

    def greet(s, _):
        pl.semaphore_signal(barrier, inc=1, device_id=(lax.rem(me + s, n),), device_id_type=MESH)
        return 0

    lax.fori_loop(1, n, greet, 0)
    for copy in weights:
        copy.start()

    experts = lax.broadcasted_iota(jnp.int32, (n, tokens), 0)
    hot0 = (experts == ids_ref[0:1, :]).astype(F32)
    hot1 = (experts == ids_ref[1:2, :]).astype(F32)
    square = (tokens, tokens)
    before = (
        lax.broadcasted_iota(jnp.int32, square, 0) < lax.broadcasted_iota(jnp.int32, square, 1)
    ).astype(F32).astype(BF16)
    earlier0 = jnp.dot(hot0.astype(BF16), before, preferred_element_type=F32)
    earlier1 = jnp.dot(hot1.astype(BF16), before, preferred_element_type=F32)
    count0 = jnp.sum(hot0, axis=1, keepdims=True)
    stride = float(cap * parts)
    base0 = jnp.sum(hot0 * earlier0, axis=0, keepdims=True) + ids_ref[0:1, :].astype(F32) * stride
    base1 = (
        jnp.sum(hot1 * (earlier1 + count0), axis=0, keepdims=True)
        + ids_ref[1:2, :].astype(F32) * stride
    )

    total = jnp.zeros((tokens, 1), F32)
    for q in range(parts):
        wide = tok_ref[:, q * part:(q + 1) * part].astype(F32)
        total += jnp.sum(wide * wide, axis=1, keepdims=True)
    inverse = lax.rsqrt(total / width + 1e-05)
    for q in range(parts):
        cut = slice(q * part, (q + 1) * part)
        normed[:, cut] = (tok_ref[:, cut].astype(F32) * inverse * gain_ref[:, cut]).astype(BF16)

    pl.semaphore_wait(barrier, n - 1)

    def out_copy(h, j):
        return pltpu.make_async_remote_copy(
            src_ref=send.at[h, j], dst_ref=recv.at[h, place],
            send_sem=s1.at[h, j], recv_sem=r1.at[h, place],
            device_id=(block_of(h) * per + j,), device_id_type=MESH,
        )

    def in_copy(h, j):
        return pltpu.make_async_remote_copy(
            src_ref=send.at[h, j], dst_ref=recv.at[h, j],
            send_sem=s1.at[h, j], recv_sem=r1.at[h, j],
            device_id=(block_of(h) * per + j,), device_id_type=MESH,
        )

    def back_copy(h, j):
        return pltpu.make_async_remote_copy(
            src_ref=yout.at[h, j], dst_ref=ret.at[h, place],
            send_sem=s2.at[h, j], recv_sem=r2.at[h, place],
            device_id=(block_of(h) * per + j,), device_id_type=MESH,
        )

    def home_copy(h, j):
        return pltpu.make_async_remote_copy(
            src_ref=yout.at[h, j], dst_ref=ret.at[h, j],
            send_sem=s2.at[h, j], recv_sem=r2.at[h, j],
            device_id=(block_of(h) * per + j,), device_id_type=MESH,
        )

    def each(h, act):
        def step(j, _):
            @pl.when(jnp.logical_or(h != 0, j != place))
            def _():
                act(j)
            return 0
        lax.fori_loop(0, per, step, 0)

    def dispatch(i, _):
        h = BLOCKS - 1 - i
        first = (block_of(h) * rows).astype(F32)
        at = lax.broadcasted_iota(jnp.int32, (rows, tokens), 0).astype(F32) + first
        picked = jnp.zeros((rows, part), F32)
        for q in range(parts):
            shift = float(q * cap)
            hot = jnp.logical_or(at == base0 + shift, at == base1 + shift)
            picked += jnp.dot(
                hot.astype(F32).astype(BF16), normed[:, q * part:(q + 1) * part],
                preferred_element_type=F32,
            )
        send[h] = picked.astype(BF16).reshape(per, cap * parts, part)
        each(h, lambda j: out_copy(h, j).start())
        return 0

    lax.fori_loop(0, BLOCKS, dispatch, 0)
    recv[0, place] = send[0, place]

    logits = lax.dot_general(
        router_ref[...], normed[...], (((1,), (1,)), ((), ())), preferred_element_type=F32
    )
    first = jnp.sum(hot0 * logits, axis=0, keepdims=True)
    second = jnp.sum(hot1 * logits, axis=0, keepdims=True)
    weight0 = to_column(jax.nn.sigmoid(first - second))
    weight1 = to_column(jax.nn.sigmoid(second - first))
    column0, column1 = to_column(base0), to_column(base1)
    acc[...] = tok_ref[...].astype(F32)
    for copy in weights:
        copy.wait()

    def ffn(i, _):
        h = BLOCKS - 1 - i
        each(h, lambda j: in_copy(h, j).wait_recv())
        xs[...] = jnp.dot(
            split_ref[...], recv[h].reshape(rows, part), preferred_element_type=F32
        ).astype(BF16)
        hidden = gate_v.shape[1]
        gate = jnp.zeros((flat, hidden), F32)
        up = jnp.zeros((flat, hidden), F32)
        for q in range(parts):
            x = xs[q * flat:(q + 1) * flat, :]
            gate += jnp.dot(x, gate_v[q * part:(q + 1) * part, :], preferred_element_type=F32)
            up += jnp.dot(x, up_v[q * part:(q + 1) * part, :], preferred_element_type=F32)
        act = (gate / (1.0 + jnp.exp(-gate)) * up).astype(BF16)
        for q in range(parts):
            ys[q * flat:(q + 1) * flat, :] = jnp.dot(
                act, down_v[:, q * part:(q + 1) * part], preferred_element_type=F32
            ).astype(BF16)
        yout[h] = jnp.dot(
            merge_ref[...], ys[...], preferred_element_type=F32
        ).astype(BF16).reshape(per, cap * parts, part)
        each(h, lambda j: back_copy(h, j).start())
        return 0

    lax.fori_loop(0, BLOCKS, ffn, 0)
    ret[0, place] = yout[0, place]

    def combine(h, _):
        each(h, lambda j: home_copy(h, j).wait_recv())
        start = (block_of(h) * rows).astype(F32)
        at = lax.broadcasted_iota(jnp.int32, (tokens, rows), 1).astype(F32) + start
        back = ret[h].reshape(rows, part)
        for q in range(parts):
            shift = float(q * cap)
            cut = slice(q * part, (q + 1) * part)
            hot_a = (at == column0 + shift).astype(F32).astype(BF16)
            hot_b = (at == column1 + shift).astype(F32).astype(BF16)
            acc[:, cut] += weight0 * jnp.dot(hot_a, back, preferred_element_type=F32)
            acc[:, cut] += weight1 * jnp.dot(hot_b, back, preferred_element_type=F32)
        return 0

    lax.fori_loop(0, BLOCKS, combine, 0)

    score = jnp.zeros((tokens, 1), F32)
    for q in range(parts):
        cut = slice(q * part, (q + 1) * part)
        mixed = acc[:, cut].astype(BF16)
        mixed_ref[:, cut] = mixed
        score += jnp.sum(
            mixed.astype(F32) * head_ref[:, cut].astype(F32), axis=1, keepdims=True
        )
    values = jnp.tanh(to_row(score))
    values_ref[...] = values
    error = values - target_ref[...].astype(F32)
    recency = recency_ref[...]
    weighted = jnp.sum(recency * error * error, axis=1, keepdims=True)
    weight = jnp.sum(recency, axis=1, keepdims=True)
    lane = lax.broadcasted_iota(jnp.int32, sums.shape, 1)
    sums[...] = jnp.where(lane == 0, weighted, jnp.where(lane == 1, weight, 0.0))
    all_sums[me] = sums[...]

    def sum_copy(to, slot):
        return pltpu.make_async_remote_copy(
            src_ref=sums, dst_ref=all_sums.at[slot],
            send_sem=s3.at[to], recv_sem=r3.at[slot],
            device_id=(to,), device_id_type=MESH,
        )

    def share(s, _):
        sum_copy(lax.rem(me + s, n), me).start()
        return 0

    lax.fori_loop(1, n, share, 0)

    def drain(h, _):
        each(h, lambda j: out_copy(h, j).wait_send())
        each(h, lambda j: back_copy(h, j).wait_send())
        return 0

    lax.fori_loop(0, BLOCKS, drain, 0)

    def take(s, _):
        other = lax.rem(me + s, n)
        sum_copy(other, other).wait_recv()
        return 0

    lax.fori_loop(1, n, take, 0)
    whole = jnp.sum(all_sums[...], axis=0)
    loss_ref[...] = whole[0:1, 0:1] / whole[0:1, 1:2]

    def leave(s, _):
        other = lax.rem(me + s, n)
        sum_copy(other, other).wait_send()
        return 0

    lax.fori_loop(1, n, leave, 0)


def body(
    axis,
    n,
    tokens,
    norm_gain,
    router_weight,
    expert_ids,
    gate_proj,
    up_proj,
    down_proj,
    value_weight,
    value_target,
    recency,
):
    count, width = tokens.shape
    hidden = gate_proj.shape[2]
    cap = 3 * count // n
    parts = 1
    while cap * parts % 16:
        parts *= 2
    part = width // parts
    per = n // BLOCKS
    rows, flat = per * cap * parts, per * cap
    order = np.arange(rows).reshape(per, parts, cap).transpose(1, 0, 2).reshape(-1)
    split = np.zeros((rows, rows), np.float32)
    split[np.arange(rows), order] = 1.0
    merge = jnp.asarray(split.T, BF16)
    split = jnp.asarray(split, BF16)
    vmem = pl.BlockSpec(memory_space=pltpu.VMEM)
    block = (BLOCKS, per, cap * parts, part)
    dma = pltpu.SemaphoreType.DMA
    mixed, values, loss = pl.pallas_call(
        functools.partial(kernel, axis, n, cap, parts),
        out_shape=(
            jax.ShapeDtypeStruct((count, width), BF16),
            jax.ShapeDtypeStruct((1, count), F32),
            jax.ShapeDtypeStruct((1, 1), F32),
        ),
        in_specs=[vmem] * 9 + [pl.BlockSpec(memory_space=pl.ANY)] * 3,
        out_specs=(vmem, vmem, vmem),
        scratch_shapes=[
            pltpu.VMEM((width, hidden), BF16),
            pltpu.VMEM((width, hidden), BF16),
            pltpu.VMEM((hidden, width), BF16),
            pltpu.VMEM((count, width), BF16),
            pltpu.VMEM(block, BF16),
            pltpu.VMEM(block, BF16),
            pltpu.VMEM((rows, part), BF16),
            pltpu.VMEM((rows, part), BF16),
            pltpu.VMEM(block, BF16),
            pltpu.VMEM(block, BF16),
            pltpu.VMEM((count, width), F32),
            pltpu.VMEM((8, 128), F32),
            pltpu.VMEM((n, 8, 128), F32),
            dma((3,)),
            dma((BLOCKS, per)),
            dma((BLOCKS, per)),
            dma((BLOCKS, per)),
            dma((BLOCKS, per)),
            dma((n,)),
            dma((n,)),
        ],
        compiler_params=pltpu.CompilerParams(
            collective_id=0, has_side_effects=True, vmem_limit_bytes=60 * 2**20
        ),
        cost_estimate=pl.CostEstimate(
            flops=6 * n * cap * width * hidden,
            bytes_accessed=6 * width * hidden,
            transcendentals=n * cap * hidden,
        ),
    )(
        tokens,
        norm_gain.reshape(1, width),
        router_weight.T,
        expert_ids.T,
        value_weight.reshape(1, width),
        value_target.reshape(1, count),
        recency.reshape(1, count),
        split,
        merge,
        gate_proj,
        up_proj,
        down_proj,
    )
    return (mixed, values.reshape(count), loss.reshape(()))


def solution(mesh):
    axis = mesh.axis_names[0]
    return jax.shard_map(
        functools.partial(body, axis, mesh.shape[axis]),
        mesh=mesh,
        in_specs=(
            P(axis, None),
            P(),
            P(),
            P(axis, None),
            P(axis, None, None),
            P(axis, None, None),
            P(axis, None, None),
            P(),
            P(axis),
            P(axis),
        ),
        out_specs=(P(axis, None), P(axis), P()),
        check_vma=False,
    )
```

time: 312 us -> 182 us (0.58)
  Pallas kernels: 0 us -> 175 us
  blocking collectives: 139 us -> 0 us
  waiting for transfers between devices: 93.2 us -> 0 us
  local copies, waits for them, and re-layouts: 38.7 us -> 4.71 us
  matrix products: 23.6 us -> 0 us
  other arithmetic: 8.31 us -> 0 us
  starting transfers between devices: 4.02 us -> 0 us
    pallas_call x0 -> x1, Pallas kernels: none -> 175 us  [body(): pl.pallas_call(functools.partial(kernel, axis, n, cap, parts), out_shape=...]
    all_to_all x1 -> x0, blocking collectives: 101 us -> none  [body(): lax.all_to_all(outgoing, 'expert', split_axis=0, concat_axis=0, tiled=True)]
    all_to_all x1 -> x0, waiting for transfers between devices: 93.2 us -> none  [body(): lax.all_to_all(produced, 'expert', split_axis=0, concat_axis=0, tiled=True)]
    psum x1 -> x0, blocking collectives: 38.2 us -> none  [body(): lax.psum((jnp.sum(recency * error * error), jnp.sum(recency)), 'expert')]
    dot_general x4 -> x0, matrix products: 23.6 us -> none  [the longest x1 14.2 us: expert_ffn(): jnp.dot(hidden, down_proj[0], preferred_element_type=jnp.float32)]
    reshape x5 -> x1, local copies, waits for them, and re-layouts: 23.7 us -> 1.31 us  [body(): value_weight.reshape(1, width)]
    gather x2 -> x0, local copies, waits for them, and re-layouts: 7.27 us -> none  [the longest x1 4.06 us: body(): outgoing = padded[source_row].reshape(expert_total, capacity, width)]
    convert_element_type x3 -> x0, other arithmetic: 5.24 us -> none  [the longest x1 4.19 us: body(): mixed = (wide + gate_first[:, None] * picked[:, 0].astype(jnp.float32) +...]
  transfers between devices with their start and end apart: 1 -> 0, of which waited for: 1 -> 0; matrix products, arithmetic and copies ran while one was open for 0% -> 0% of each run, Pallas kernels for 0% -> 0%
where the time goes in v1:
time: 182 us
  Pallas kernels  175 us (96%)
  local copies, waits for them, and re-layouts  4.71 us (3%)
  between operations  2.4 us (1%)
    pallas_call x1, Pallas kernels, body(): pl.pallas_call(functools.partial(kernel, axis, n, cap, parts), out_shape=...  175 us

profile of v1, /device:TPU:0, one launch (start us, length us, event | category | flops | bytes accessed | tf_op | source)
XLA Modules:
  0.0 182.2 jit_solution(12243695702523258067)
XLA Ops:
  0.6 1.3 reshape.25.head_ref
  1.9 175.1 %shard_map.139 = (bf16[128,4096]{1,0:T(8,128)(2,1)}, f32[1,128]{1,0:T(1,128)}, f32[1,1]{1,0:T(1,128)}) custom-call(bf16[128,4096]{1,0:T(8,128)(2,1)} %tok_ref.1, f32[1,4096]{1,0:T(1,128)} %bitcast.8, bf16[32,4096]{1,0:T(8,128)(2,1)} %bitcast.7, s32[2,128]{1,0:T(2,128)} %bitcast.9, bf16[1,4096]{1,0:T(2,128)(2,1)} %reshape.25.head_ref, s32[1,128]{1,0:T(1,128)} %bitcast.10, ...), custom_call_target="tpu_custom_call" | custom-call | flops 7247757312 | bytes 18874368 | tf_op jit(solution)/shard_map/pallas_call | solution.py:291
  177.0 2.3 %copy.18 = bf16[128,4096]{1,0:T(8,128)(2,1)} copy(bf16[128,4096]{1,0:T(8,128)(2,1)} %get-tuple-element.12) | data formatting | bytes 2097152
  179.3 1.1 copy.19

commit v2 on v1

--- a/solution.py
+++ b/solution.py
@@ -9,6 +9,9 @@
 from jax.sharding import PartitionSpec as P
 
 BLOCKS = 4
+SENT = (2, 3, 1, 0)
+WORKED = (2, 3, 1, 0)
+TAKEN = (2, 0, 1, 3)
 MESH = pl.DeviceIdType.MESH
 F32 = jnp.float32
 BF16 = jnp.bfloat16
@@ -120,8 +123,13 @@
             device_id=(block_of(h) * per + j,), device_id_type=MESH,
         )
 
+    def pick(order, i):
+        return sum(jnp.where(i == k, h, 0) for k, h in enumerate(order))
+
     def each(h, act):
-        def step(j, _):
+        def step(turn, _):
+            j = lax.rem(place + turn, per)
+
             @pl.when(jnp.logical_or(h != 0, j != place))
             def _():
                 act(j)
@@ -129,7 +137,7 @@
         lax.fori_loop(0, per, step, 0)
 
     def dispatch(i, _):
-        h = BLOCKS - 1 - i
+        h = pick(SENT, i)
         first = (block_of(h) * rows).astype(F32)
         at = lax.broadcasted_iota(jnp.int32, (rows, tokens), 0).astype(F32) + first
         picked = jnp.zeros((rows, part), F32)
@@ -160,7 +168,7 @@
         copy.wait()
 
     def ffn(i, _):
-        h = BLOCKS - 1 - i
+        h = pick(WORKED, i)
         each(h, lambda j: in_copy(h, j).wait_recv())
         xs[...] = jnp.dot(
             split_ref[...], recv[h].reshape(rows, part), preferred_element_type=F32
@@ -186,7 +194,8 @@
     lax.fori_loop(0, BLOCKS, ffn, 0)
     ret[0, place] = yout[0, place]
 
-    def combine(h, _):
+    def combine(i, _):
+        h = pick(TAKEN, i)
         each(h, lambda j: home_copy(h, j).wait_recv())
         start = (block_of(h) * rows).astype(F32)
         at = lax.broadcasted_iota(jnp.int32, (tokens, rows), 1).astype(F32) + start

time: 182 us -> 166 us (0.912)
  Pallas kernels: 175 us -> 158 us
    pallas_call x1, Pallas kernels: 175 us -> 158 us  [body(): pl.pallas_call(functools.partial(kernel, axis, n, cap, parts), out_shape=...]
where the time goes in v2:
time: 166 us; the launch traced here: 165 us
  Pallas kernels  158 us (95%)
  local copies, waits for them, and re-layouts  4.71 us (3%)
  between operations  2.4 us (1%)
    pallas_call x1, Pallas kernels, body(): pl.pallas_call(functools.partial(kernel, axis, n, cap, parts), out_shape=...  158 us
    unnamed x2, local copies, waits for them, and re-layouts  3.4 us

profile of v2, /device:TPU:0, one launch (start us, length us, event | category | flops | bytes accessed | tf_op | source)
XLA Modules:
  0.0 165.3 jit_solution(10251809102840993444)
XLA Ops:
  0.6 1.3 reshape.25.head_ref
  1.9 158.2 %shard_map.139 = (bf16[128,4096]{1,0:T(8,128)(2,1)}, f32[1,128]{1,0:T(1,128)}, f32[1,1]{1,0:T(1,128)}) custom-call(bf16[128,4096]{1,0:T(8,128)(2,1)} %tok_ref.1, f32[1,4096]{1,0:T(1,128)} %bitcast.8, bf16[32,4096]{1,0:T(8,128)(2,1)} %bitcast.7, s32[2,128]{1,0:T(2,128)} %bitcast.9, bf16[1,4096]{1,0:T(2,128)(2,1)} %reshape.25.head_ref, s32[1,128]{1,0:T(1,128)} %bitcast.10, ...), custom_call_target="tpu_custom_call" | custom-call | flops 7247757312 | bytes 18874368 | tf_op jit(solution)/shard_map/pallas_call | solution.py:300
  160.2 2.3 %copy.18 = bf16[128,4096]{1,0:T(8,128)(2,1)} copy(bf16[128,4096]{1,0:T(8,128)(2,1)} %get-tuple-element.12) | data formatting | bytes 2097152
  162.5 1.1 copy.19

commit v3 on v2

--- a/solution.py
+++ b/solution.py
@@ -211,14 +211,18 @@
 
     lax.fori_loop(0, BLOCKS, combine, 0)
 
+    head = head_ref[...].astype(F32)
+    lanes = head.shape[1]
     score = jnp.zeros((tokens, 1), F32)
     for q in range(parts):
         cut = slice(q * part, (q + 1) * part)
         mixed = acc[:, cut].astype(BF16)
         mixed_ref[:, cut] = mixed
-        score += jnp.sum(
-            mixed.astype(F32) * head_ref[:, cut].astype(F32), axis=1, keepdims=True
-        )
+        partial = jnp.zeros((tokens, lanes), F32)
+        for k in range(part // lanes):
+            row = q * (part // lanes) + k
+            partial += mixed[:, k * lanes:(k + 1) * lanes].astype(F32) * head[row:row + 1, :]
+        score += jnp.sum(partial, axis=1, keepdims=True)
     values = jnp.tanh(to_row(score))
     values_ref[...] = values
     error = values - target_ref[...].astype(F32)
@@ -341,7 +345,7 @@
         norm_gain.reshape(1, width),
         router_weight.T,
         expert_ids.T,
-        value_weight.reshape(1, width),
+        value_weight.reshape(width // 128, 128),
         value_target.reshape(1, count),
         recency.reshape(1, count),
         split,

time: 166 us -> 164 us (0.988)
  no operation moved by 1% of the time
where the time goes in v3:
time: 164 us
  Pallas kernels  158 us (96%)
  local copies, waits for them, and re-layouts  3.4 us (2%)
  between operations  2.41 us (1%)
    pallas_call x1, Pallas kernels, body(): pl.pallas_call(functools.partial(kernel, axis, n, cap, parts), out_shape=...  158 us
    unnamed x2, local copies, waits for them, and re-layouts  3.4 us

profile of v3, /device:TPU:0, one launch (start us, length us, event | category | flops | bytes accessed | tf_op | source)
XLA Modules:
  0.0 164.0 jit_solution(8335329818894348407)
XLA Ops:
  0.6 158.2 %shard_map.139 = (bf16[128,4096]{1,0:T(8,128)(2,1)}, f32[1,128]{1,0:T(1,128)}, f32[1,1]{1,0:T(1,128)}) custom-call(bf16[128,4096]{1,0:T(8,128)(2,1)} %tok_ref.1, f32[1,4096]{1,0:T(1,128)} %bitcast.9, bf16[32,4096]{1,0:T(8,128)(2,1)} %bitcast.8, s32[2,128]{1,0:T(2,128)} %bitcast.11, bf16[32,128]{1,0:T(8,128)(2,1)} %bitcast.10, s32[1,128]{1,0:T(1,128)} %bitcast.12, ...), custom_call_target="tpu_custom_call" | custom-call | flops 7247757312 | bytes 18874368 | tf_op jit(solution)/shard_map/pallas_call | solution.py:304
  158.9 2.3 %copy.18 = bf16[128,4096]{1,0:T(8,128)(2,1)} copy(bf16[128,4096]{1,0:T(8,128)(2,1)} %get-tuple-element.12) | data formatting | bytes 2097152
  161.2 1.1 copy.19
